TPU v7x, 256 devices: a whole 4x4x8 slice. The times are simulated.
256 devices in a mesh: dp: 32 (over y, z), mp: 8 (over x, core).
Axes of the slice: x: 4, y: 4, z: 8, core: 2. Of those that a mesh axis runs over, the one named last changes fastest.
Arguments:
- grads: bfloat16 [768, 512, 512], P('dp', 'mp'), may hold values from -6 to 6
- owner_slot: int32 [768], P('dp'), may hold values from 0 to 767, as said below
- refresh_flag: int32 [768], P(('dp', 'mp')), may hold values from 0 to 1, as said below
- left_stats: bfloat16 [768, 512, 512], P(('dp', 'mp')), may hold values from -1 to 16, as said below
- right_stats: bfloat16 [768, 512, 512], P(('dp', 'mp')), may hold values from -1 to 16, as said below
- left_root: bfloat16 [768, 512, 512], P(('dp', 'mp')), may hold values from -1 to 1, as said below
- right_root: bfloat16 [768, 512, 512], P(('dp', 'mp')), may hold values from -1 to 1, as said below
Outputs:
- left_new: bfloat16 [768, 512, 512], P(('dp', 'mp'))
- right_new: bfloat16 [768, 512, 512], P(('dp', 'mp'))
- direction: bfloat16 [768, 512, 512], P(('dp', 'mp'))
Inputs may be any that keep to these rules, and one draw needn't show every extreme that they name: `owner_slot`: A permutation of the slots. Slot s lies on the device that is number s // 3 in dp-major order. The 24 blocks of one dp index go to exactly 2 slots of each owner dp index s // 24 that they reach, and each owner dp index receives exactly 24 blocks. Every dp index d sends blocks to the owner dp indices d + 1 and d + 16, counted round. `refresh_flag`: exactly 48 ones; at most one on a device, and at most one on the two devices with mp indices 2i and 2i + 1 of one dp index. `left_stats`: each block symmetric positive definite. `right_stats`: each block symmetric positive definite. `left_root`: each block symmetric positive definite. `right_root`: each block symmetric positive definite.
All inputs are finite; a program needn't handle non-finite values.
Results may differ from a plain program's by a relative error of at most 0.0051.
Values may be sent and summed in bfloat16 or wider, within the bound.
A program may use at most 64 MiB of HBM per device.

v0:
```python
import functools

import jax
import jax.numpy as jnp
from jax import lax
from jax.experimental import pallas as pl
from jax.experimental.pallas import tpu as pltpu
from jax.sharding import PartitionSpec as P

decay_rate = 0.9


def multiply(first_op, second_op):
    return jnp.dot(first_op, second_op, preferred_element_type=jnp.float32)


def iota2(shape, axis):
    return lax.broadcasted_iota(jnp.int32, shape, axis)


def total_of(mask, values):
    return jnp.max(jnp.where(mask, values, 0), keepdims=True)


def long_need(ones, twos, threes, fours):
    odd = twos & 1
    rest = jnp.maximum(ones - threes - 2 * odd, 0)
    lanes = fours + threes + ((twos + 1) >> 1) + ((rest + 3) >> 2)
    spare = ones - threes
    used = jnp.where(
        rest > 0,
        jnp.where((rest & 3) == 0, 4, rest & 3),
        jnp.where(
            twos > 0,
            jnp.where(odd == 1, 2 + jnp.clip(spare, 0, 2), 4),
            jnp.where(threes > 0, jnp.where(spare >= 0, 4, 3), 4),
        ),
    )
    return jnp.where(lanes > 0, 4 * (lanes - 1) + used, 0)


def long_plan(counts, hop, rank):
    n1, n2, n3, n4, n5, n6, n7 = counts
    best, split = long_need(n1, n2, n3, 0 * n4), 0 * n4
    best = jnp.maximum(best, long_need(n7, n6, n5, n4))
    for c in range(1, 5):
        other = jnp.maximum(long_need(n1, n2, n3, 0 * n4 + c), long_need(n7, n6, n5, jnp.maximum(n4 - c, 0)))
        better = (n4 >= c) & (other < best)
        best, split = jnp.where(better, other, best), jnp.where(better, c, split)
    plus = (hop < 4) | ((hop == 4) & (rank < split))
    length = jnp.where(plus, hop, 8 - hop)
    index = jnp.where((hop == 4) & (rank >= split), rank - split, rank)
    twos, threes = jnp.where(plus, n2, n6), jnp.where(plus, n3, n5)
    fours = jnp.where(plus, split, n4 - split)
    odd = twos & 1
    spare = index - threes
    rest = spare - 2 * odd
    lane1 = jnp.where(
        spare < 0,
        fours + index,
        jnp.where(rest < 0, fours + threes + (twos >> 1), fours + threes + ((twos + 1) >> 1) + (rest >> 2)),
    )
    start1 = jnp.where(spare < 0, 3, jnp.where(rest < 0, 2 + spare, rest & 3))
    lane = jnp.where(
        length == 4,
        index,
        jnp.where(length == 3, fours + index, jnp.where(length == 2, fours + threes + (index >> 1), lane1)),
    )
    start = jnp.where(length >= 3, 0, jnp.where(length == 2, 2 * (index & 1), start1))
    first = jnp.where(plus, 0, 32) + 4 * lane + start
    return first, first + length - 1, best


def short_plan(counts, hop, rank):
    m1, m2, m3 = counts
    best, split = jnp.maximum(m1, 2 * m2 + m3), 0 * m2
    for c in range(1, 9):
        other = jnp.maximum(2 * c + m1, 2 * (m2 - c) + m3)
        better = (m2 >= c) & (other < best)
        best, split = jnp.where(better, other, best), jnp.where(better, c, split)
    plus = (hop == 1) | ((hop == 2) & (rank < split))
    index = jnp.where((hop == 2) & (rank >= split), rank - split, rank)
    twos = jnp.where(plus, split, m2 - split)
    lane = jnp.where(hop == 2, index, twos + (index >> 1))
    start = jnp.where(hop == 2, 0, index & 1)
    first = jnp.where(plus, 0, 16) + 2 * lane + start
    return first, first + jnp.where(hop == 2, 1, 0), best


def plan(owner, me):
    square = (32, 32)
    source, target = iota2(square, 0), iota2(square, 1)
    ys, zs, yt, zt = source >> 3, source & 7, target >> 3, target & 7
    along_y, along_z = (yt - ys) & 3, (zt - zs) & 7
    seen = jnp.zeros(square, jnp.int32)
    held, label = [seen, seen], [seen, seen]
    for b in range(24):
        inside = owner[:, b : b + 1] - 24 * target
        match = (inside >= 0) & (inside < 24)
        for p in range(2):
            now = match & (seen == p)
            held[p] = held[p] + jnp.where(now, b, 0)
            label[p] = label[p] + jnp.where(now, inside, 0)
        seen = seen + match.astype(jnp.int32)
    present = seen > 0
    flags = present.astype(jnp.float32)

    def count(first_op, second_op):
        return jnp.dot(first_op, second_op, preferred_element_type=jnp.float32).astype(jnp.int32)

    def mask(condition):
        return condition.astype(jnp.float32)

    same_z, same_y = zs == zt, ys == yt
    rank_az, many_az = count(flags, mask(same_z & (ys < yt))), count(flags, mask(same_z))
    rank_by, many_by = count(flags, mask(same_y & (zs < zt))), count(flags, mask(same_y))
    rank_ay, many_ay = count(mask(same_y & (zt < zs)), flags), count(mask(same_y), flags)
    rank_bz, many_bz = count(mask(same_z & (yt < ys)), flags), count(mask(same_z), flags)
    first_az, last_az, need_az = long_plan([total_of(along_z == k, many_az) for k in range(1, 8)], along_z, rank_az)
    first_bz, last_bz, need_bz = long_plan([total_of(along_z == k, many_bz) for k in range(1, 8)], along_z, rank_bz)
    first_ay, last_ay, need_ay = short_plan([total_of(along_y == k, many_ay) for k in range(1, 4)], along_y, rank_ay)
    first_by, last_by, need_by = short_plan([total_of(along_y == k, many_by) for k in range(1, 4)], along_y, rank_by)

    lanes = iota2((1, 64), 1)
    diagonal = source == target

    def standing(row):
        return jnp.sum(jnp.where(diagonal, row, 0), axis=1, keepdims=True)

    def table(place, values):
        at, value = standing(place), standing(values)
        return jnp.sum(jnp.where(at == lanes, value + 1, 0), axis=0, keepdims=True) - 1

    def own_row(values):
        return jnp.sum(jnp.where(source == me, values, 0), axis=0, keepdims=True)

    my_y, my_z = me >> 3, me & 7
    rows = []
    place = own_row(jnp.where(present & (along_z > 0), first_az, -1))
    rows += [table(place, own_row(held[p])) for p in range(2)]
    place = own_row(jnp.where(present & (along_y > 0), first_by, -1))
    rows += [table(place, own_row(held[p])) for p in range(2)]

    spread_y, spread_z = mask(ys == yt), mask(zs == zt)

    def condense(keep, values, spread, pick):
        moved = count(jnp.where(keep, values, 0).astype(jnp.float32), spread)
        return jnp.sum(jnp.where(pick, moved, 0), axis=0, keepdims=True)

    keep = present & (along_y > 0) & (ys == my_y) & (zt == my_z)
    pick = (ys == my_y) & (zs == zt)
    place = condense(keep, first_ay + 1, spread_y, pick) - 1
    for p in range(2):
        code = jnp.where(along_z == 0, held[p], 32 + last_az)
        rows.append(table(place, condense(keep, code, spread_y, pick)))
    keep = present & (along_z > 0) & (zs == my_z) & (yt == my_y)
    pick = (zs == my_z) & (ys == yt)
    place = condense(keep, first_bz + 1, spread_z, pick) - 1
    for p in range(2):
        code = jnp.where(along_y == 0, held[p], 32 + last_by)
        rows.append(table(place, condense(keep, code, spread_z, pick)))

    def column(values):
        return jnp.sum(jnp.where(target == me, values, 0), axis=1, keepdims=True)

    for first_axis, second_axis, last_one, last_two in ((along_z, along_y, last_az, last_ay), (along_y, along_z, last_by, last_bz)):
        row = jnp.zeros((1, 64), jnp.int32)
        for p in range(2):
            code = jnp.where(
                second_axis > 0,
                160 + 2 * last_two + p,
                jnp.where(first_axis > 0, 32 + 2 * last_one + p, held[p]),
            )
            at, value = column(jnp.where(present, label[p] + 1, 0)) - 1, column(code)
            row = row + jnp.sum(jnp.where(at == lanes, value, 0), axis=0, keepdims=True)
        rows.append(row)
    return rows, jnp.maximum(need_az, need_bz), jnp.maximum(need_ay, need_by)


MESH = pl.DeviceIdType.MESH
BUILDS = ((10, 10), (11, 10), (12, 10), (13, 11), (14, 11), (16, 12), (20, 12), (32, 16))


def along(axis, distance):
    dp = lax.axis_index("dp")
    if axis == "z":
        return ((dp // 8) * 8 + (dp + distance) % 8, lax.axis_index("mp"))
    return ((dp + 8 * distance) % 32, lax.axis_index("mp"))


def meet(devices):
    barrier = pltpu.get_barrier_semaphore()
    for device in devices:
        pl.semaphore_signal(barrier, inc=1, device_id=device, device_id_type=MESH)
    pl.semaphore_wait(barrier, len(devices))


def plan_kernel(slots_ref, table_ref, owner, send_sem, recv_sem):
    dp = lax.axis_index("dp")
    column, row = dp % 8, dp // 8
    ring_z = [along("z", k) for k in range(1, 8)]
    ring_y = [along("y", k) for k in range(1, 4)]
    owner[pl.ds(dp, 1)] = slots_ref[...]
    meet(ring_z + ring_y)
    copies = []
    for k, device in enumerate(ring_z):
        copies.append(
            pltpu.make_async_remote_copy(
                src_ref=owner.at[pl.ds(dp, 1)],
                dst_ref=owner.at[pl.ds(dp, 1)],
                send_sem=send_sem.at[k],
                recv_sem=recv_sem.at[k],
                device_id=device,
                device_id_type=MESH,
            )
        )
        copies[-1].start()
    for copy in copies:
        copy.wait_recv()
    for k, device in enumerate(ring_y):
        copies.append(
            pltpu.make_async_remote_copy(
                src_ref=owner.at[pl.ds(8 * row, 8)],
                dst_ref=owner.at[pl.ds(8 * row, 8)],
                send_sem=send_sem.at[7 + k],
                recv_sem=recv_sem.at[7 + k],
                device_id=device,
                device_id_type=MESH,
            )
        )
        copies[-1].start()
    for copy in copies[7:]:
        copy.wait_recv()
    for copy in copies:
        copy.wait_send()
    rows, need_z, need_y = plan(owner[...].reshape(32, 128), dp)
    for k, entries in enumerate(rows):
        table_ref[k : k + 1, 0:64] = entries
    build = jnp.zeros((1, 1), jnp.int32)
    for steps_z, steps_y in BUILDS[:-1]:
        build = build + jnp.where((need_z > steps_z) | (need_y > steps_y), 1, 0)
    table_ref[10:11, 0:64] = jnp.broadcast_to(build, (1, 64))


def make_plan(owner_slot):
    slots = jnp.pad(owner_slot, (0, 128 - owner_slot.shape[0])).reshape(1, 1, 128)
    return pl.pallas_call(
        plan_kernel,
        out_shape=jax.ShapeDtypeStruct((16, 128), jnp.int32),
        in_specs=[pl.BlockSpec(memory_space=pltpu.VMEM)],
        out_specs=pl.BlockSpec(memory_space=pltpu.VMEM),
        scratch_shapes=[
            pltpu.VMEM((32, 1, 128), jnp.int32),
            pltpu.SemaphoreType.DMA((10,)),
            pltpu.SemaphoreType.DMA((10,)),
        ],
        compiler_params=pltpu.CompilerParams(collective_id=0, has_side_effects=True),
        name="plan",
    )(slots)


class Lanes:
    def __init__(self, axis, steps, rows, columns, table, own, before, sent, got, send_sem, recv_sem):
        self.length, self.half = (4, 32) if axis == "z" else (2, 16)
        self.axis, self.steps, self.rows, self.columns = axis, steps, rows, columns
        self.table, self.own, self.before, self.sent, self.got = table, own, before, sent, got
        self.send_sem, self.recv_sem = send_sem, recv_sem

    def value(self, place, p, step):
        code = self.table[self.rows + p, place]
        fresh = self.own[jnp.clip(code, 0, 23), :, self.columns]
        if self.before is not None:
            earlier = self.before[jnp.clip(2 * (code - 32) + p, 0, self.before.shape[0] - 1)]
            fresh = jnp.where(code < 32, fresh, earlier)
        if step == 0:
            return fresh
        return jnp.where(code >= 0, fresh, self.got[2 * (place - 1) + p])

    def copy(self, place, way):
        return pltpu.make_async_remote_copy(
            src_ref=self.sent.at[pl.ds(2 * place, 2)],
            dst_ref=self.got.at[pl.ds(2 * place, 2)],
            send_sem=self.send_sem.at[place],
            recv_sem=self.recv_sem.at[place],
            device_id=along(self.axis, 1 - 2 * way),
            device_id_type=MESH,
        )

    def each(self, step, action):
        lanes = (self.steps - step + self.length - 1) // self.length

        def body(lane, carry):
            for way in range(2):
                action(way * self.half + lane * self.length + step, way)
            return carry

        lax.fori_loop(0, lanes, body, 0)

    def step(self, step):
        def action(place, way):
            if step > 0:
                self.copy(place - 1, way).wait_recv()
            for p in range(2):
                self.sent[2 * place + p] = self.value(place, p, step)
            self.copy(place, way).start()

        self.each(step, action)

    def arrive(self):
        def body(lane, carry):
            for way in range(2):
                self.copy(way * self.half + lane * self.length + self.length - 1, way).wait_recv()
            return carry

        whole, part = self.steps // self.length, self.steps % self.length
        lax.fori_loop(0, whole, body, 0)
        if part:
            for way in range(2):
                self.copy(way * self.half + whole * self.length + part - 1, way).wait_recv()

    def close(self):
        for step in range(self.length):
            self.each(step, lambda place, way: self.copy(place, way).wait_send())


def exchange_kernel(steps_z, steps_y, table, grads, blocks, own, *scratch):
    sent_az, got_az, sent_ay, got_ay, sent_by, got_by, sent_bz, got_bz, pack_a, pack_b = scratch[:10]
    sem_az, sem_ay, sem_by, sem_bz, mp_send, mp_recv, local_sem = scratch[10:]
    mp = lax.axis_index("mp")
    dp = lax.axis_index("dp")
    load = pltpu.make_async_copy(grads, own, local_sem.at[0])
    load.start()
    meet([along("z", 1), along("z", -1), along("y", 1), along("y", -1)] + [(dp, (mp + k) % 8) for k in range(1, 8)])
    load.wait()
    width = own.shape[2] // 2
    left, right = pl.ds(0, width), pl.ds(width, width)
    az = Lanes("z", steps_z, 0, left, table, own, None, sent_az, got_az, sem_az.at[0], sem_az.at[1])
    by = Lanes("y", steps_y, 2, right, table, own, None, sent_by, got_by, sem_by.at[0], sem_by.at[1])
    ay = Lanes("y", steps_y, 4, left, table, own, got_az, sent_ay, got_ay, sem_ay.at[0], sem_ay.at[1])
    bz = Lanes("z", steps_z, 6, right, table, own, got_by, sent_bz, got_bz, sem_bz.at[0], sem_bz.at[1])
    pending = []

    def deliver(row, columns, first, second, pack, number):
        def body(slot, carry):
            code = table[row, slot]
            pack[slot] = jnp.where(
                code < 32,
                own[jnp.clip(code, 0, 23), :, columns],
                jnp.where(
                    code < 160,
                    first[jnp.clip(code - 32, 0, first.shape[0] - 1)],
                    second[jnp.clip(code - 160, 0, second.shape[0] - 1)],
                ),
            )
            return carry

        lax.fori_loop(0, own.shape[0], body, 0)
        place = blocks.at[:, pl.ds(pl.multiple_of(64 * mp, 64), 64), columns]
        for k in range(1, 8):
            peer = (mp + k) % 8
            copy = pltpu.make_async_remote_copy(
                src_ref=pack.at[pl.ds(3 * peer, 3)],
                dst_ref=place,
                send_sem=mp_send.at[number, k],
                recv_sem=mp_recv.at[number, k],
                device_id=(dp, peer),
                device_id_type=MESH,
            )
            copy.start()
            pending.append(copy)
        copy = pltpu.make_async_copy(pack.at[pl.ds(3 * mp, 3)], place, local_sem.at[1 + number])
        copy.start()
        pending.append(copy)

    for step in range(4):
        az.step(step)
        if step < 2:
            by.step(step)
    by.arrive()
    bz.step(0)
    az.arrive()
    ay.step(0)
    bz.step(1)
    ay.step(1)
    bz.step(2)
    ay.arrive()
    deliver(8, left, got_az, got_ay, pack_a, 0)
    bz.step(3)
    bz.arrive()
    deliver(9, right, got_by, got_bz, pack_b, 1)
    for copy in pending:
        copy.wait()
    for lanes in (az, by, ay, bz):
        lanes.close()


def exchange(number, table, grads):
    steps_z, steps_y = BUILDS[number]
    held, rows, columns = grads.shape
    half = columns // 2
    long, short = pltpu.VMEM((128, rows, half), jnp.bfloat16), pltpu.VMEM((64, rows, half), jnp.bfloat16)
    return pl.pallas_call(
        functools.partial(exchange_kernel, steps_z, steps_y),
        out_shape=jax.ShapeDtypeStruct((3, columns, columns), jnp.bfloat16),
        in_specs=[pl.BlockSpec(memory_space=pltpu.SMEM), pl.BlockSpec(memory_space=pl.ANY)],
        out_specs=pl.BlockSpec(memory_space=pl.ANY),
        scratch_shapes=[
            pltpu.VMEM(grads.shape, jnp.bfloat16),
            long,
            long,
            short,
            short,
            short,
            short,
            long,
            long,
            pltpu.VMEM((held, rows, half), jnp.bfloat16),
            pltpu.VMEM((held, rows, half), jnp.bfloat16),
            pltpu.SemaphoreType.DMA((2, 64)),
            pltpu.SemaphoreType.DMA((2, 32)),
            pltpu.SemaphoreType.DMA((2, 32)),
            pltpu.SemaphoreType.DMA((2, 64)),
            pltpu.SemaphoreType.DMA((2, 8)),
            pltpu.SemaphoreType.DMA((2, 8)),
            pltpu.SemaphoreType.DMA((3,)),
        ],
        compiler_params=pltpu.CompilerParams(
            collective_id=1 + number, has_side_effects=True, vmem_limit_bytes=56 << 20
        ),
        name=f"exchange_{steps_z}_{steps_y}",
    )(table, grads)


def newton_root(matrix):
    size = matrix.shape[0]
    identity = (
        lax.broadcasted_iota(jnp.int32, (size, size), 0) == lax.broadcasted_iota(jnp.int32, (size, size), 1)
    ).astype(jnp.float32)
    wide = matrix.astype(jnp.float32)
    scaling = 2.5 / jnp.sqrt(jnp.sum(wide * wide) + 1e-06)
    scaled = scaling * wide
    squared = (scaling * scaling) * multiply(matrix, matrix)
    shift = (squared - 10.0 * scaled) * 0.0625
    half_shift = shift.astype(jnp.bfloat16)
    quartic = 3.125 * shift + multiply(half_shift, half_shift)
    through = (5.0 * scaled - squared) * 0.25
    fifth = 2.44140625 * through + multiply(quartic.astype(jnp.bfloat16), through.astype(jnp.bfloat16))
    offset = -0.3125 * scaled - 0.25 * fifth
    half_offset = offset.astype(jnp.bfloat16)
    doubled = 3.125 * offset + multiply(half_offset, half_offset)
    half_doubled = doubled.astype(jnp.bfloat16)
    fourth = 4.8828125 * doubled + multiply(half_doubled, half_doubled)
    carried = 1.5625 * scaled + scaling * multiply(half_offset, matrix)
    last = 5.9604644775390625 * carried + multiply(fourth.astype(jnp.bfloat16), carried.astype(jnp.bfloat16))
    root = 1.953125 * identity + 1.25 * offset - 0.25 * last
    return (jnp.sqrt(jnp.sqrt(scaling)) * root).astype(jnp.bfloat16)


def update_kernel(flag_ref, grad_ref, left_ref, right_ref, left_root_ref, right_root_ref, left_out, right_out, dir_out, use_left, use_right):
    slot = pl.program_id(0)
    block = grad_ref[0]
    gram_left = lax.dot_general(block, block, (((1,), (1,)), ((), ())), preferred_element_type=jnp.float32)
    left_out[0] = (decay_rate * left_ref[0].astype(jnp.float32) + (1.0 - decay_rate) * gram_left).astype(jnp.bfloat16)
    gram_right = lax.dot_general(block, block, (((0,), (0,)), ((), ())), preferred_element_type=jnp.float32)
    right_out[0] = (decay_rate * right_ref[0].astype(jnp.float32) + (1.0 - decay_rate) * gram_right).astype(jnp.bfloat16)

    @pl.when(flag_ref[slot] > 0)
    def _():
        use_left[...] = newton_root(left_out[0])
        use_right[...] = newton_root(right_out[0])

    @pl.when(flag_ref[slot] <= 0)
    def _():
        use_left[...] = left_root_ref[0]
        use_right[...] = right_root_ref[0]

    half_way = multiply(use_left[...], block).astype(jnp.bfloat16)
    preconditioned = multiply(half_way, use_right[...])
    wide = block.astype(jnp.float32)
    grad_norm = jnp.sum(wide * wide)
    dir_norm = jnp.sum(preconditioned * preconditioned)
    dir_out[0] = (preconditioned * jnp.sqrt(grad_norm / (dir_norm + 1e-06))).astype(jnp.bfloat16)


def update(refresh_flag, blocks, left_stats, right_stats, left_root, right_root):
    slots, size = blocks.shape[0], blocks.shape[1]
    spec = pl.BlockSpec((1, size, size), lambda k: (k, 0, 0))
    return pl.pallas_call(
        update_kernel,
        grid=(slots,),
        in_specs=[pl.BlockSpec(memory_space=pltpu.SMEM)] + [spec] * 5,
        out_specs=[spec] * 3,
        out_shape=[jax.ShapeDtypeStruct(blocks.shape, jnp.bfloat16)] * 3,
        scratch_shapes=[pltpu.VMEM((size, size), jnp.bfloat16)] * 2,
        compiler_params=pltpu.CompilerParams(vmem_limit_bytes=56 << 20),
        name="update",
    )(refresh_flag, blocks, left_stats, right_stats, left_root, right_root)


def local(grads, owner_slot, refresh_flag, left_stats, right_stats, left_root, right_root):
    table = make_plan(owner_slot)
    builds = [functools.partial(exchange, number) for number in range(len(BUILDS))]
    blocks = lax.switch(table[10, 0], builds, table, grads)
    return tuple(update(refresh_flag, blocks, left_stats, right_stats, left_root, right_root))


def solution(mesh):
    placed = (
        P("dp", "mp", None),
        P("dp"),
        P(("dp", "mp")),
        P(("dp", "mp"), None, None),
        P(("dp", "mp"), None, None),
        P(("dp", "mp"), None, None),
        P(("dp", "mp"), None, None),
    )
    return jax.shard_map(
        local,
        mesh=mesh,
        in_specs=placed,
        out_specs=(
            P(("dp", "mp"), None, None),
            P(("dp", "mp"), None, None),
            P(("dp", "mp"), None, None),
        ),
        check_vma=False,
    )
```

profile of v0, /device:TPU:1, one launch (start us, length us, event | category | flops | bytes accessed | tf_op | source)
XLA Modules:
  0.0 99.1 jit_solution(18077982089867055929)
XLA Ops:
  0.6 1.2 %pad_bitcast_fusion.slots_ref = s32[1,1,128]{2,1,0:T(1,128)} fusion(s32[24]{0:T(128)} %param.16), kind=kLoop, calls=%fused_computation | loop fusion | bytes 608 | tf_op jit(solution)/shard_map/reshape | solution.py:246
  1.8 18.3 %plan.1 = s32[16,128]{1,0:T(8,128)S(1)} custom-call(s32[1,1,128]{2,1,0:T(1,128)} %pad_bitcast_fusion.slots_ref), custom_call_target="tpu_custom_call" | custom-call | tf_op jit(solution)/shard_map/plan/pallas_call | solution.py:247
  20.1 0.5 slice.3
  21.3 63.7 %conditional.1 = (bf16[3,512,512]{2,1,0:T(8,128)(2,1)S(1)}) conditional(s32[]{:T(128)} %bitcast.1, (s32[16,128]{1,0:T(8,128)S(1)}, bf16[24,64,512]{2,1,0:T(8,128)(2,1)}) %tuple.31, (s32[16,128]{1,0:T(8,128)S(1)}, bf16[24,64,512]{2,1,0:T(8,128)(2,1)}) %tuple.31, (s32[16,128]{1,0:T(8,128)S(1)}, ...), branch_computations={%region_0.1_spmd, %region_1.2_spmd, %region_2.3_spmd, %region_3.4_... | conditional | bytes 8 | solution.py:503
  21.3 63.4 %exchange_12_10.1 = bf16[3,512,512]{2,1,0:T(8,128)(2,1)S(1)} custom-call(s32[16,128]{1,0:T(8,128)S(1)} %get-tuple-element.42.table, bf16[24,64,512]{2,1,0:T(8,128)(2,1)} %get-tuple-element.43.grads), custom_call_target="tpu_custom_call" | custom-call | tf_op jit(solution)/shard_map/cond/branch_2_fun/exchange_12_10/pallas_call | solution.py:402
  85.0 14.1 %update.1 = (bf16[3,512,512]{2,1,0:T(8,128)(2,1)}, bf16[3,512,512]{2,1,0:T(8,128)(2,1)}, bf16[3,512,512]{2,1,0:T(8,128)(2,1)}) custom-call(s32[3]{0:T(128)} %flag_ref.1, bf16[3,512,512]{2,1,0:T(8,128)(2,1)S(1)} %get-tuple-element.60.grad_ref, bf16[3,512,512]{2,1,0:T(8,128)(2,1)} %left_ref.1, bf16[3,512,512]{2,1,0:T(8,128)(2,1)} %right_ref.1, ...), custom_call_target="tpu_custom_call" | custom-call | tf_op jit(solution)/shard_map/update/pallas_call | solution.py:488
where the time goes:
time: 99.2 us; the launch traced here: 99.1 us
  Pallas kernels  95.8 us (97%)
  local copies, waits for them, and re-layouts  1.68 us (2%)
  between operations  1.3 us (1%)
    pallas_call x1, Pallas kernels, exchange(): pl.pallas_call(functools.partial(exchange_kernel, steps_z, steps_y), out_...  63.4 us
    pallas_call x1, Pallas kernels, make_plan(): pl.pallas_call(plan_kernel, out_shape=jax.ShapeDtypeStruct((16, 128), jnp...  18.3 us
    pallas_call x1, Pallas kernels, update(): pl.pallas_call(update_kernel, grid=(slots,), in_specs=[pl.BlockSpec(memor...  14.1 us

commit v1 on v0

--- a/solution.py
+++ b/solution.py
@@ -178,7 +178,7 @@
 
 
 MESH = pl.DeviceIdType.MESH
-BUILDS = ((10, 10), (11, 10), (12, 10), (13, 11), (14, 11), (16, 12), (20, 12), (32, 16))
+BUILDS = ((10, 9), (12, 8), (12, 9), (14, 9), (14, 11), (16, 10), (20, 12), (32, 16))
 
 
 def along(axis, distance):
@@ -195,9 +195,9 @@
     pl.semaphore_wait(barrier, len(devices))
 
 
-def plan_kernel(slots_ref, table_ref, owner, send_sem, recv_sem):
+def plan_kernel(slots_ref, table_ref, build_ref, owner, send_sem, recv_sem):
     dp = lax.axis_index("dp")
-    column, row = dp % 8, dp // 8
+    row = dp // 8
     ring_z = [along("z", k) for k in range(1, 8)]
     ring_y = [along("y", k) for k in range(1, 4)]
     owner[pl.ds(dp, 1)] = slots_ref[...]
@@ -236,19 +236,21 @@
     rows, need_z, need_y = plan(owner[...].reshape(32, 128), dp)
     for k, entries in enumerate(rows):
         table_ref[k : k + 1, 0:64] = entries
-    build = jnp.zeros((1, 1), jnp.int32)
-    for steps_z, steps_y in BUILDS[:-1]:
-        build = build + jnp.where((need_z > steps_z) | (need_y > steps_y), 1, 0)
-    table_ref[10:11, 0:64] = jnp.broadcast_to(build, (1, 64))
+    build = jnp.full((1, 1), len(BUILDS) - 1, jnp.int32)
+    for number in range(len(BUILDS) - 2, -1, -1):
+        steps_z, steps_y = BUILDS[number]
+        build = jnp.where((need_z <= steps_z) & (need_y <= steps_y), number, build)
+    build_ref[...] = build
 
 
 def make_plan(owner_slot):
     slots = jnp.pad(owner_slot, (0, 128 - owner_slot.shape[0])).reshape(1, 1, 128)
+    vmem = pl.BlockSpec(memory_space=pltpu.VMEM)
     return pl.pallas_call(
         plan_kernel,
-        out_shape=jax.ShapeDtypeStruct((16, 128), jnp.int32),
-        in_specs=[pl.BlockSpec(memory_space=pltpu.VMEM)],
-        out_specs=pl.BlockSpec(memory_space=pltpu.VMEM),
+        out_shape=[jax.ShapeDtypeStruct((16, 128), jnp.int32), jax.ShapeDtypeStruct((1, 1), jnp.int32)],
+        in_specs=[vmem],
+        out_specs=[vmem, vmem],
         scratch_shapes=[
             pltpu.VMEM((32, 1, 128), jnp.int32),
             pltpu.SemaphoreType.DMA((10,)),
@@ -260,170 +262,249 @@
 
 
 class Lanes:
-    def __init__(self, axis, steps, rows, columns, table, own, before, sent, got, send_sem, recv_sem):
-        self.length, self.half = (4, 32) if axis == "z" else (2, 16)
-        self.axis, self.steps, self.rows, self.columns = axis, steps, rows, columns
-        self.table, self.own, self.before, self.sent, self.got = table, own, before, sent, got
-        self.send_sem, self.recv_sem = send_sem, recv_sem
-
-    def value(self, place, p, step):
-        code = self.table[self.rows + p, place]
+    def __init__(self, near, steps, rows, columns, table, own, before, buffers, sems):
+        self.near, self.length, self.half = near
+        self.steps, self.rows, self.columns = steps, rows, columns
+        self.table, self.own, self.before = table, own, before
+        self.sent, self.got = buffers
+        self.send_sem, self.recv_sem = sems
+
+    def received(self, entry, columns):
+        unused = jnp.where(entry >= 2 * self.half, 2 * (self.half - self.steps), 0)
+        return self.got[jnp.clip(entry - unused, 0, 4 * self.steps - 1), :, columns]
+
+    def value(self, way, at, p, step):
+        code = self.table[self.rows + p, way * self.half + at]
         fresh = self.own[jnp.clip(code, 0, 23), :, self.columns]
         if self.before is not None:
-            earlier = self.before[jnp.clip(2 * (code - 32) + p, 0, self.before.shape[0] - 1)]
-            fresh = jnp.where(code < 32, fresh, earlier)
+            lanes, columns = self.before
+            fresh = jnp.where(code < 32, fresh, lanes.received(2 * (code - 32) + p, columns))
         if step == 0:
             return fresh
-        return jnp.where(code >= 0, fresh, self.got[2 * (place - 1) + p])
-
-    def copy(self, place, way):
+        return jnp.where(code >= 0, fresh, self.got[2 * (way * self.steps + at - 1) + p])
+
+    def copy(self, way, at):
+        plus, minus = self.near
+        place = way * self.steps + at
         return pltpu.make_async_remote_copy(
             src_ref=self.sent.at[pl.ds(2 * place, 2)],
             dst_ref=self.got.at[pl.ds(2 * place, 2)],
-            send_sem=self.send_sem.at[place],
+            send_sem=self.send_sem.at[0],
             recv_sem=self.recv_sem.at[place],
-            device_id=along(self.axis, 1 - 2 * way),
+            device_id=(plus + way * (minus - plus), lax.axis_index("mp")),
             device_id_type=MESH,
         )
 
     def each(self, step, action):
         lanes = (self.steps - step + self.length - 1) // self.length
 
-        def body(lane, carry):
-            for way in range(2):
-                action(way * self.half + lane * self.length + step, way)
+        def body(number, carry):
+            action(number % 2, number // 2 * self.length + step)
             return carry
 
-        lax.fori_loop(0, lanes, body, 0)
+        lax.fori_loop(0, 2 * lanes, body, 0)
+
+    def fill(self, way, at, step):
+        for p in range(2):
+            self.sent[2 * (way * self.steps + at) + p] = self.value(way, at, p, step)
+
+    def ready(self):
+        self.each(0, lambda way, at: self.fill(way, at, 0))
+
+    def leave(self):
+        self.each(0, lambda way, at: self.copy(way, at).start())
 
     def step(self, step):
-        def action(place, way):
+        def action(way, at):
             if step > 0:
-                self.copy(place - 1, way).wait_recv()
-            for p in range(2):
-                self.sent[2 * place + p] = self.value(place, p, step)
-            self.copy(place, way).start()
+                self.copy(way, at - 1).wait_recv()
+            self.fill(way, at, step)
+            self.copy(way, at).start()
 
         self.each(step, action)
 
     def arrive(self):
-        def body(lane, carry):
-            for way in range(2):
-                self.copy(way * self.half + lane * self.length + self.length - 1, way).wait_recv()
+        whole, part = self.steps // self.length, self.steps % self.length
+
+        def body(number, carry):
+            lane = number // 2
+            last = jnp.where(lane < whole, self.length, part) - 1
+            self.copy(number % 2, lane * self.length + last).wait_recv()
             return carry
 
-        whole, part = self.steps // self.length, self.steps % self.length
-        lax.fori_loop(0, whole, body, 0)
-        if part:
-            for way in range(2):
-                self.copy(way * self.half + whole * self.length + part - 1, way).wait_recv()
+        lax.fori_loop(0, 2 * (whole + (part > 0)), body, 0)
 
     def close(self):
-        for step in range(self.length):
-            self.each(step, lambda place, way: self.copy(place, way).wait_send())
+        pltpu.make_async_remote_copy(
+            src_ref=self.sent,
+            dst_ref=self.got,
+            send_sem=self.send_sem.at[0],
+            recv_sem=self.recv_sem.at[0],
+            device_id=(self.near[0], lax.axis_index("mp")),
+            device_id_type=MESH,
+        ).wait_send()
 
 
 def exchange_kernel(steps_z, steps_y, table, grads, blocks, own, *scratch):
-    sent_az, got_az, sent_ay, got_ay, sent_by, got_by, sent_bz, got_bz, pack_a, pack_b = scratch[:10]
-    sem_az, sem_ay, sem_by, sem_bz, mp_send, mp_recv, local_sem = scratch[10:]
+    buffers_by = scratch[0:2]
+    buffers_az, buffers_ay, buffers_bz = ((scratch[k : k + 2], scratch[k + 2 : k + 4]) for k in (2, 6, 10))
+    packs = scratch[14]
+    sems = [(scratch[15 + 2 * k], scratch[16 + 2 * k]) for k in range(7)]
+    mp_send, mp_recv, local_sem = scratch[29:]
     mp = lax.axis_index("mp")
     dp = lax.axis_index("dp")
-    load = pltpu.make_async_copy(grads, own, local_sem.at[0])
+    load = pltpu.make_async_copy(grads, own, local_sem.at[4])
     load.start()
-    meet([along("z", 1), along("z", -1), along("y", 1), along("y", -1)] + [(dp, (mp + k) % 8) for k in range(1, 8)])
+    barrier = pltpu.get_barrier_semaphore()
+    row = (dp // 8) * 8
+    near_z = (row + (dp + 1) % 8, row + (dp + 7) % 8)
+    near_y = ((dp + 8) % 32, (dp + 24) % 32)
+    for device in near_z + near_y:
+        pl.semaphore_signal(barrier, inc=1, device_id=(device, mp), device_id_type=MESH)
+
+    def greet(k, carry):
+        pl.semaphore_signal(barrier, inc=1, device_id=(dp, (mp + k) % 8), device_id_type=MESH)
+        return carry
+
+    lax.fori_loop(1, 8, greet, 0)
+    half = own.shape[2] // 2
+    quarter = half // 2
+    quarters = [pl.ds(k * quarter, quarter) for k in range(4)]
+    by = Lanes((near_y, 2, 16), steps_y, 2, pl.ds(half, half), table, own, None, buffers_by, sems[0])
+    az1, az2 = (
+        Lanes((near_z, 4, 32), steps_z, 0, quarters[k], table, own, None, buffers_az[k], sems[1 + k])
+        for k in range(2)
+    )
+    ay1, ay2 = (
+        Lanes((near_y, 2, 16), steps_y, 4, quarters[k], table, own, ((az1, az2)[k], quarters[0]), buffers_ay[k], sems[3 + k])
+        for k in range(2)
+    )
+    bz1, bz2 = (
+        Lanes((near_z, 4, 32), steps_z, 6, quarters[2 + k], table, own, (by, quarters[k]), buffers_bz[k], sems[5 + k])
+        for k in range(2)
+    )
     load.wait()
-    width = own.shape[2] // 2
-    left, right = pl.ds(0, width), pl.ds(width, width)
-    az = Lanes("z", steps_z, 0, left, table, own, None, sent_az, got_az, sem_az.at[0], sem_az.at[1])
-    by = Lanes("y", steps_y, 2, right, table, own, None, sent_by, got_by, sem_by.at[0], sem_by.at[1])
-    ay = Lanes("y", steps_y, 4, left, table, own, got_az, sent_ay, got_ay, sem_ay.at[0], sem_ay.at[1])
-    bz = Lanes("z", steps_z, 6, right, table, own, got_by, sent_bz, got_bz, sem_bz.at[0], sem_bz.at[1])
-    pending = []
-
-    def deliver(row, columns, first, second, pack, number):
+    az1.ready()
+    pl.semaphore_wait(barrier, 11)
+
+    def place(number):
+        return blocks.at[:, pl.ds(pl.multiple_of(64 * mp, 64), 64), quarters[number]]
+
+    def spread(number, k):
+        peer = (mp + k) % 8
+        return pltpu.make_async_remote_copy(
+            src_ref=packs.at[number, pl.ds(3 * peer, 3)],
+            dst_ref=place(number),
+            send_sem=mp_send.at[number],
+            recv_sem=mp_recv.at[number, k],
+            device_id=(dp, peer),
+            device_id_type=MESH,
+        )
+
+    def keep(number):
+        return pltpu.make_async_copy(packs.at[number, pl.ds(3 * mp, 3)], place(number), local_sem.at[number])
+
+    def deliver(row, number, lanes):
+        columns = quarters[number]
+        first, first_columns = lanes.before
+
         def body(slot, carry):
             code = table[row, slot]
-            pack[slot] = jnp.where(
+            packs[number, slot] = jnp.where(
                 code < 32,
                 own[jnp.clip(code, 0, 23), :, columns],
                 jnp.where(
                     code < 160,
-                    first[jnp.clip(code - 32, 0, first.shape[0] - 1)],
-                    second[jnp.clip(code - 160, 0, second.shape[0] - 1)],
+                    first.received(code - 32, first_columns),
+                    lanes.received(code - 160, quarters[0]),
                 ),
             )
             return carry
 
         lax.fori_loop(0, own.shape[0], body, 0)
-        place = blocks.at[:, pl.ds(pl.multiple_of(64 * mp, 64), 64), columns]
-        for k in range(1, 8):
-            peer = (mp + k) % 8
-            copy = pltpu.make_async_remote_copy(
-                src_ref=pack.at[pl.ds(3 * peer, 3)],
-                dst_ref=place,
-                send_sem=mp_send.at[number, k],
-                recv_sem=mp_recv.at[number, k],
-                device_id=(dp, peer),
-                device_id_type=MESH,
-            )
-            copy.start()
-            pending.append(copy)
-        copy = pltpu.make_async_copy(pack.at[pl.ds(3 * mp, 3)], place, local_sem.at[1 + number])
-        copy.start()
-        pending.append(copy)
-
-    for step in range(4):
-        az.step(step)
-        if step < 2:
-            by.step(step)
+        def send(k, carry):
+            spread(number, k).start()
+            return carry
+
+        lax.fori_loop(1, 8, send, 0)
+        keep(number).start()
+
+    az1.leave()
+    az2.step(0)
+    by.step(0)
+    az1.step(1)
+    az2.step(1)
+    by.step(1)
+    az1.step(2)
+    az2.step(2)
+    az1.step(3)
+    az2.step(3)
     by.arrive()
-    bz.step(0)
-    az.arrive()
-    ay.step(0)
-    bz.step(1)
-    ay.step(1)
-    bz.step(2)
-    ay.arrive()
-    deliver(8, left, got_az, got_ay, pack_a, 0)
-    bz.step(3)
-    bz.arrive()
-    deliver(9, right, got_by, got_bz, pack_b, 1)
-    for copy in pending:
-        copy.wait()
-    for lanes in (az, by, ay, bz):
+    bz1.step(0)
+    az1.arrive()
+    ay1.step(0)
+    bz2.step(0)
+    az2.arrive()
+    ay1.step(1)
+    ay2.step(0)
+    bz1.step(1)
+    bz2.step(1)
+    ay1.arrive()
+    deliver(8, 0, ay1)
+    ay2.step(1)
+    bz1.step(2)
+    bz2.step(2)
+    ay2.arrive()
+    deliver(8, 1, ay2)
+    bz1.step(3)
+    bz2.step(3)
+    bz1.arrive()
+    deliver(9, 2, bz1)
+    bz2.arrive()
+    deliver(9, 3, bz2)
+    for number in range(4):
+
+        def settle(k, carry):
+            spread(number, k).wait_recv()
+            return carry
+
+        lax.fori_loop(1, 8, settle, 0)
+        pltpu.make_async_remote_copy(
+            src_ref=packs.at[number, pl.ds(0, 21)],
+            dst_ref=packs.at[number, pl.ds(0, 21)],
+            send_sem=mp_send.at[number],
+            recv_sem=mp_recv.at[number, 1],
+            device_id=(dp, (mp + 1) % 8),
+            device_id_type=MESH,
+        ).wait_send()
+        keep(number).wait()
+    for lanes in (by, az1, az2, ay1, ay2, bz1, bz2):
         lanes.close()
 
 
 def exchange(number, table, grads):
     steps_z, steps_y = BUILDS[number]
     held, rows, columns = grads.shape
-    half = columns // 2
-    long, short = pltpu.VMEM((128, rows, half), jnp.bfloat16), pltpu.VMEM((64, rows, half), jnp.bfloat16)
+
+    def buffers(steps, parts):
+        return [pltpu.VMEM((4 * steps, rows, columns // parts), jnp.bfloat16)] * 2
+
+    def sems(*steps):
+        return [pltpu.SemaphoreType.DMA((size,)) for count in steps for size in (1, 2 * count)]
+
     return pl.pallas_call(
         functools.partial(exchange_kernel, steps_z, steps_y),
         out_shape=jax.ShapeDtypeStruct((3, columns, columns), jnp.bfloat16),
         in_specs=[pl.BlockSpec(memory_space=pltpu.SMEM), pl.BlockSpec(memory_space=pl.ANY)],
         out_specs=pl.BlockSpec(memory_space=pl.ANY),
-        scratch_shapes=[
-            pltpu.VMEM(grads.shape, jnp.bfloat16),
-            long,
-            long,
-            short,
-            short,
-            short,
-            short,
-            long,
-            long,
-            pltpu.VMEM((held, rows, half), jnp.bfloat16),
-            pltpu.VMEM((held, rows, half), jnp.bfloat16),
-            pltpu.SemaphoreType.DMA((2, 64)),
-            pltpu.SemaphoreType.DMA((2, 32)),
-            pltpu.SemaphoreType.DMA((2, 32)),
-            pltpu.SemaphoreType.DMA((2, 64)),
-            pltpu.SemaphoreType.DMA((2, 8)),
-            pltpu.SemaphoreType.DMA((2, 8)),
-            pltpu.SemaphoreType.DMA((3,)),
-        ],
+        scratch_shapes=[pltpu.VMEM(grads.shape, jnp.bfloat16)]
+        + buffers(steps_y, 2)
+        + buffers(steps_z, 4) * 2
+        + buffers(steps_y, 4) * 2
+        + buffers(steps_z, 4) * 2
+        + [pltpu.VMEM((4, held, rows, columns // 4), jnp.bfloat16)]
+        + sems(steps_y, steps_z, steps_z, steps_y, steps_y, steps_z, steps_z)
+        + [pltpu.SemaphoreType.DMA((4,)), pltpu.SemaphoreType.DMA((4, 8)), pltpu.SemaphoreType.DMA((5,))],
         compiler_params=pltpu.CompilerParams(
             collective_id=1 + number, has_side_effects=True, vmem_limit_bytes=56 << 20
         ),
@@ -498,9 +579,9 @@
 
 
 def local(grads, owner_slot, refresh_flag, left_stats, right_stats, left_root, right_root):
-    table = make_plan(owner_slot)
+    table, build = make_plan(owner_slot)
     builds = [functools.partial(exchange, number) for number in range(len(BUILDS))]
-    blocks = lax.switch(table[10, 0], builds, table, grads)
+    blocks = lax.switch(build[0, 0], builds, table, grads)
     return tuple(update(refresh_flag, blocks, left_stats, right_stats, left_root, right_root))
 
 

time: 99.2 us -> 92.9 us (0.936)
  the two profiles are of different devices: /device:TPU:1 before, /device:TPU:7 now
where the time goes in v1:
time: 92.9 us; the launch traced here: 92.8 us
  Pallas kernels  90 us (97%)
  between operations  1.28 us (1%)
  local copies, waits for them, and re-layouts  1.17 us (1%)
    pallas_call x1, Pallas kernels, exchange(): pl.pallas_call(functools.partial(exchange_kernel, steps_z, steps_y), out_...  58.1 us
    pallas_call x1, Pallas kernels, make_plan(): pl.pallas_call(plan_kernel, out_shape=[jax.ShapeDtypeStruct((16, 128), jn...  17.8 us
    pallas_call x1, Pallas kernels, update(): pl.pallas_call(update_kernel, grid=(slots,), in_specs=[pl.BlockSpec(memor...  14.1 us

profile of v1, /device:TPU:7, one launch (start us, length us, event | category | flops | bytes accessed | tf_op | source)
XLA Modules:
  0.0 92.8 jit_solution(18243258387340601412)
XLA Ops:
  0.6 1.2 %pad_bitcast_fusion.slots_ref = s32[1,1,128]{2,1,0:T(1,128)} fusion(s32[24]{0:T(128)} %param.16), kind=kLoop, calls=%fused_computation | loop fusion | bytes 608 | tf_op jit(solution)/shard_map/reshape | solution.py:247
  1.8 17.8 %plan.1 = (s32[16,128]{1,0:T(8,128)S(1)}, s32[1,1]{1,0:T(1,128)}) custom-call(s32[1,1,128]{2,1,0:T(1,128)} %pad_bitcast_fusion.slots_ref), custom_call_target="tpu_custom_call" | custom-call | tf_op jit(solution)/shard_map/plan/pallas_call | solution.py:249
  20.3 58.4 %conditional.1 = (bf16[3,512,512]{2,1,0:T(8,128)(2,1)S(1)}) conditional(s32[]{:T(128)} %bitcast.1, (s32[16,128]{1,0:T(8,128)S(1)}, bf16[24,64,512]{2,1,0:T(8,128)(2,1)}) %tuple.31, (s32[16,128]{1,0:T(8,128)S(1)}, bf16[24,64,512]{2,1,0:T(8,128)(2,1)}) %tuple.31, (s32[16,128]{1,0:T(8,128)S(1)}, ...), branch_computations={%region_0.1_spmd, %region_1.2_spmd, %region_2.3_spmd, %region_3.4_... | conditional | bytes 8 | solution.py:584
  20.3 58.1 %exchange_14_9.1 = bf16[3,512,512]{2,1,0:T(8,128)(2,1)S(1)} custom-call(s32[16,128]{1,0:T(8,128)S(1)} %get-tuple-element.44.table, bf16[24,64,512]{2,1,0:T(8,128)(2,1)} %get-tuple-element.48.grads), custom_call_target="tpu_custom_call" | custom-call | tf_op jit(solution)/shard_map/cond/branch_3_fun/exchange_14_9/pallas_call | solution.py:495
  78.7 14.1 %update.1 = (bf16[3,512,512]{2,1,0:T(8,128)(2,1)}, bf16[3,512,512]{2,1,0:T(8,128)(2,1)}, bf16[3,512,512]{2,1,0:T(8,128)(2,1)}) custom-call(s32[3]{0:T(128)} %flag_ref.1, bf16[3,512,512]{2,1,0:T(8,128)(2,1)S(1)} %get-tuple-element.64.grad_ref, bf16[3,512,512]{2,1,0:T(8,128)(2,1)} %left_ref.1, bf16[3,512,512]{2,1,0:T(8,128)(2,1)} %right_ref.1, ...), custom_call_target="tpu_custom_call" | custom-call | tf_op jit(solution)/shard_map/update/pallas_call | solution.py:569

commit v2 on v1

--- a/solution.py
+++ b/solution.py
@@ -39,14 +39,18 @@
     return jnp.where(lanes > 0, 4 * (lanes - 1) + used, 0)
 
 
-def long_plan(counts, hop, rank):
+def long_share(counts):
     n1, n2, n3, n4, n5, n6, n7 = counts
-    best, split = long_need(n1, n2, n3, 0 * n4), 0 * n4
-    best = jnp.maximum(best, long_need(n7, n6, n5, n4))
+    best, split = jnp.maximum(long_need(n1, n2, n3, 0 * n4), long_need(n7, n6, n5, n4)), 0 * n4
     for c in range(1, 5):
         other = jnp.maximum(long_need(n1, n2, n3, 0 * n4 + c), long_need(n7, n6, n5, jnp.maximum(n4 - c, 0)))
         better = (n4 >= c) & (other < best)
         best, split = jnp.where(better, other, best), jnp.where(better, c, split)
+    return split, best
+
+
+def long_plan(counts, split, hop, rank):
+    n1, n2, n3, n4, n5, n6, n7 = counts
     plus = (hop < 4) | ((hop == 4) & (rank < split))
     length = jnp.where(plus, hop, 8 - hop)
     index = jnp.where((hop == 4) & (rank >= split), rank - split, rank)
@@ -68,23 +72,28 @@
     )
     start = jnp.where(length >= 3, 0, jnp.where(length == 2, 2 * (index & 1), start1))
     first = jnp.where(plus, 0, 32) + 4 * lane + start
-    return first, first + length - 1, best
-
-
-def short_plan(counts, hop, rank):
+    return first, first + length - 1
+
+
+def short_share(counts):
     m1, m2, m3 = counts
     best, split = jnp.maximum(m1, 2 * m2 + m3), 0 * m2
     for c in range(1, 9):
         other = jnp.maximum(2 * c + m1, 2 * (m2 - c) + m3)
         better = (m2 >= c) & (other < best)
         best, split = jnp.where(better, other, best), jnp.where(better, c, split)
+    return split, best
+
+
+def short_plan(counts, split, hop, rank):
+    m1, m2, m3 = counts
     plus = (hop == 1) | ((hop == 2) & (rank < split))
     index = jnp.where((hop == 2) & (rank >= split), rank - split, rank)
     twos = jnp.where(plus, split, m2 - split)
     lane = jnp.where(hop == 2, index, twos + (index >> 1))
     start = jnp.where(hop == 2, 0, index & 1)
     first = jnp.where(plus, 0, 16) + 2 * lane + start
-    return first, first + jnp.where(hop == 2, 1, 0), best
+    return first, first + jnp.where(hop == 2, 1, 0)
 
 
 def plan(owner, me):
@@ -92,34 +101,38 @@
     source, target = iota2(square, 0), iota2(square, 1)
     ys, zs, yt, zt = source >> 3, source & 7, target >> 3, target & 7
     along_y, along_z = (yt - ys) & 3, (zt - zs) & 7
-    seen = jnp.zeros(square, jnp.int32)
-    held, label = [seen, seen], [seen, seen]
+    both, later = jnp.zeros(square, jnp.int32), jnp.full(square, -1, jnp.int32)
     for b in range(24):
         inside = owner[:, b : b + 1] - 24 * target
         match = (inside >= 0) & (inside < 24)
-        for p in range(2):
-            now = match & (seen == p)
-            held[p] = held[p] + jnp.where(now, b, 0)
-            label[p] = label[p] + jnp.where(now, inside, 0)
-        seen = seen + match.astype(jnp.int32)
-    present = seen > 0
-    flags = present.astype(jnp.float32)
+        entry = inside + 32 * b
+        both = both + jnp.where(match, entry, 0)
+        later = jnp.where(match, entry, later)
+    present = later >= 0
+    entries = [both - later, later]
+    held, label = [entry >> 5 for entry in entries], [entry & 31 for entry in entries]
+    flags = jnp.where(present, 1.0, 0.0).astype(jnp.bfloat16)
 
     def count(first_op, second_op):
         return jnp.dot(first_op, second_op, preferred_element_type=jnp.float32).astype(jnp.int32)
 
     def mask(condition):
-        return condition.astype(jnp.float32)
+        return jnp.where(condition, 1.0, 0.0).astype(jnp.bfloat16)
 
     same_z, same_y = zs == zt, ys == yt
     rank_az, many_az = count(flags, mask(same_z & (ys < yt))), count(flags, mask(same_z))
     rank_by, many_by = count(flags, mask(same_y & (zs < zt))), count(flags, mask(same_y))
     rank_ay, many_ay = count(mask(same_y & (zt < zs)), flags), count(mask(same_y), flags)
     rank_bz, many_bz = count(mask(same_z & (yt < ys)), flags), count(mask(same_z), flags)
-    first_az, last_az, need_az = long_plan([total_of(along_z == k, many_az) for k in range(1, 8)], along_z, rank_az)
-    first_bz, last_bz, need_bz = long_plan([total_of(along_z == k, many_bz) for k in range(1, 8)], along_z, rank_bz)
-    first_ay, last_ay, need_ay = short_plan([total_of(along_y == k, many_ay) for k in range(1, 4)], along_y, rank_ay)
-    first_by, last_by, need_by = short_plan([total_of(along_y == k, many_by) for k in range(1, 4)], along_y, rank_by)
+    many_z, many_y = jnp.maximum(many_az, many_bz), jnp.maximum(many_ay, many_by)
+    counts_z = [total_of(along_z == k, many_z) for k in range(1, 8)]
+    counts_y = [total_of(along_y == k, many_y) for k in range(1, 4)]
+    split_z, need_z = long_share(counts_z)
+    split_y, need_y = short_share(counts_y)
+    first_az, last_az = long_plan(counts_z, split_z, along_z, rank_az)
+    first_bz, last_bz = long_plan(counts_z, split_z, along_z, rank_bz)
+    first_ay, last_ay = short_plan(counts_y, split_y, along_y, rank_ay)
+    first_by, last_by = short_plan(counts_y, split_y, along_y, rank_by)
 
     lanes = iota2((1, 64), 1)
     diagonal = source == target
@@ -144,7 +157,7 @@
     spread_y, spread_z = mask(ys == yt), mask(zs == zt)
 
     def condense(keep, values, spread, pick):
-        moved = count(jnp.where(keep, values, 0).astype(jnp.float32), spread)
+        moved = count(jnp.where(keep, values, 0).astype(jnp.float32).astype(jnp.bfloat16), spread)
         return jnp.sum(jnp.where(pick, moved, 0), axis=0, keepdims=True)
 
     keep = present & (along_y > 0) & (ys == my_y) & (zt == my_z)
@@ -174,11 +187,11 @@
             at, value = column(jnp.where(present, label[p] + 1, 0)) - 1, column(code)
             row = row + jnp.sum(jnp.where(at == lanes, value, 0), axis=0, keepdims=True)
         rows.append(row)
-    return rows, jnp.maximum(need_az, need_bz), jnp.maximum(need_ay, need_by)
+    return rows, need_z, need_y
 
 
 MESH = pl.DeviceIdType.MESH
-BUILDS = ((10, 9), (12, 8), (12, 9), (14, 9), (14, 11), (16, 10), (20, 12), (32, 16))
+BUILDS = ((10, 9), (12, 9), (14, 9), (14, 11), (16, 11), (32, 16))
 
 
 def along(axis, distance):
@@ -200,7 +213,7 @@
     row = dp // 8
     ring_z = [along("z", k) for k in range(1, 8)]
     ring_y = [along("y", k) for k in range(1, 4)]
-    owner[pl.ds(dp, 1)] = slots_ref[...]
+    owner[pl.ds(dp, 1), :, 0 : slots_ref.shape[2]] = slots_ref[...]
     meet(ring_z + ring_y)
     copies = []
     for k, device in enumerate(ring_z):
@@ -244,7 +257,7 @@
 
 
 def make_plan(owner_slot):
-    slots = jnp.pad(owner_slot, (0, 128 - owner_slot.shape[0])).reshape(1, 1, 128)
+    slots = owner_slot.reshape(1, 1, owner_slot.shape[0])
     vmem = pl.BlockSpec(memory_space=pltpu.VMEM)
     return pl.pallas_call(
         plan_kernel,
@@ -408,25 +421,27 @@
         columns = quarters[number]
         first, first_columns = lanes.before
 
-        def body(slot, carry):
-            code = table[row, slot]
-            packs[number, slot] = jnp.where(
-                code < 32,
-                own[jnp.clip(code, 0, 23), :, columns],
-                jnp.where(
-                    code < 160,
-                    first.received(code - 32, first_columns),
-                    lanes.received(code - 160, quarters[0]),
-                ),
-            )
-            return carry
-
-        lax.fori_loop(0, own.shape[0], body, 0)
+        def sort(peer):
+            for k in range(3):
+                slot = 3 * peer + k
+                code = table[row, slot]
+                packs[number, slot] = jnp.where(
+                    code < 32,
+                    own[jnp.clip(code, 0, 23), :, columns],
+                    jnp.where(
+                        code < 160,
+                        first.received(code - 32, first_columns),
+                        lanes.received(code - 160, quarters[0]),
+                    ),
+                )
+
         def send(k, carry):
+            sort((mp + k) % 8)
             spread(number, k).start()
             return carry
 
         lax.fori_loop(1, 8, send, 0)
+        sort(mp)
         keep(number).start()
 
     az1.leave()
@@ -512,29 +527,38 @@
     )(table, grads)
 
 
-def newton_root(matrix):
-    size = matrix.shape[0]
-    identity = (
-        lax.broadcasted_iota(jnp.int32, (size, size), 0) == lax.broadcasted_iota(jnp.int32, (size, size), 1)
-    ).astype(jnp.float32)
-    wide = matrix.astype(jnp.float32)
-    scaling = 2.5 / jnp.sqrt(jnp.sum(wide * wide) + 1e-06)
-    scaled = scaling * wide
-    squared = (scaling * scaling) * multiply(matrix, matrix)
-    shift = (squared - 10.0 * scaled) * 0.0625
-    half_shift = shift.astype(jnp.bfloat16)
-    quartic = 3.125 * shift + multiply(half_shift, half_shift)
-    through = (5.0 * scaled - squared) * 0.25
-    fifth = 2.44140625 * through + multiply(quartic.astype(jnp.bfloat16), through.astype(jnp.bfloat16))
-    offset = -0.3125 * scaled - 0.25 * fifth
-    half_offset = offset.astype(jnp.bfloat16)
-    doubled = 3.125 * offset + multiply(half_offset, half_offset)
-    half_doubled = doubled.astype(jnp.bfloat16)
-    fourth = 4.8828125 * doubled + multiply(half_doubled, half_doubled)
-    carried = 1.5625 * scaled + scaling * multiply(half_offset, matrix)
-    last = 5.9604644775390625 * carried + multiply(fourth.astype(jnp.bfloat16), carried.astype(jnp.bfloat16))
-    root = 1.953125 * identity + 1.25 * offset - 0.25 * last
-    return (jnp.sqrt(jnp.sqrt(scaling)) * root).astype(jnp.bfloat16)
+def newton_roots(*matrices):
+    size = matrices[0].shape[0]
+    diagonal = lax.broadcasted_iota(jnp.int32, (size, size), 0) == lax.broadcasted_iota(jnp.int32, (size, size), 1)
+
+    def narrow(values):
+        return [value.astype(jnp.bfloat16) for value in values]
+
+    def products(first_ops, second_ops):
+        return [multiply(one, two) for one, two in zip(first_ops, second_ops)]
+
+    wide = [matrix.astype(jnp.float32) for matrix in matrices]
+    scalings = [2.5 / jnp.sqrt(jnp.sum(value * value) + 1e-06) for value in wide]
+    scaled = [scaling * value for scaling, value in zip(scalings, wide)]
+    squared = [(scaling * scaling) * value for scaling, value in zip(scalings, products(matrices, matrices))]
+    shift = [(two - 10.0 * one) * 0.0625 for one, two in zip(scaled, squared)]
+    through = [(5.0 * one - two) * 0.25 for one, two in zip(scaled, squared)]
+    half_shift = narrow(shift)
+    quartic = [3.125 * one + two for one, two in zip(shift, products(half_shift, half_shift))]
+    fifth = [2.44140625 * one + two for one, two in zip(through, products(narrow(quartic), narrow(through)))]
+    offset = [-0.3125 * one - 0.25 * two for one, two in zip(scaled, fifth)]
+    half_offset = narrow(offset)
+    doubled = [3.125 * one + two for one, two in zip(offset, products(half_offset, half_offset))]
+    half_doubled = narrow(doubled)
+    carried = [
+        1.5625 * one + scaling * two for scaling, one, two in zip(scalings, scaled, products(half_offset, matrices))
+    ]
+    fourth = [4.8828125 * one + two for one, two in zip(doubled, products(half_doubled, half_doubled))]
+    last = [5.9604644775390625 * one + two for one, two in zip(carried, products(narrow(fourth), narrow(carried)))]
+    return [
+        (jnp.sqrt(jnp.sqrt(scaling)) * (jnp.where(diagonal, 1.953125, 0.0) + 1.25 * one - 0.25 * two)).astype(jnp.bfloat16)
+        for scaling, one, two in zip(scalings, offset, last)
+    ]
 
 
 def update_kernel(flag_ref, grad_ref, left_ref, right_ref, left_root_ref, right_root_ref, left_out, right_out, dir_out, use_left, use_right):
@@ -547,8 +571,7 @@
 
     @pl.when(flag_ref[slot] > 0)
     def _():
-        use_left[...] = newton_root(left_out[0])
-        use_right[...] = newton_root(right_out[0])
+        use_left[...], use_right[...] = newton_roots(left_out[0], right_out[0])
 
     @pl.when(flag_ref[slot] <= 0)
     def _():

time: 92.9 us -> 93.8 us (level)
  the two profiles are of different devices: /device:TPU:7 before, /device:TPU:1 now
where the time goes in v2:
time: 93.8 us; the launch traced here: 93.7 us
  Pallas kernels  92.2 us (98%)
  between operations  1.28 us (1%)
    pallas_call x1, Pallas kernels, exchange(): pl.pallas_call(functools.partial(exchange_kernel, steps_z, steps_y), out_...  60.8 us
    pallas_call x1, Pallas kernels, make_plan(): pl.pallas_call(plan_kernel, out_shape=[jax.ShapeDtypeStruct((16, 128), jn...  18 us
    pallas_call x1, Pallas kernels, update(): pl.pallas_call(update_kernel, grid=(slots,), in_specs=[pl.BlockSpec(memor...  13.4 us

profile of v2, /device:TPU:1, one launch (start us, length us, event | category | flops | bytes accessed | tf_op | source)
XLA Modules:
  0.0 93.7 jit_solution(17671230313459155211)
XLA Ops:
  0.6 18.0 %plan.1 = (s32[16,128]{1,0:T(8,128)S(1)}, s32[1,1]{1,0:T(1,128)}) custom-call(s32[1,1,24]{2,1,0:T(1,128)} %bitcast.2), custom_call_target="tpu_custom_call" | custom-call | tf_op jit(solution)/shard_map/plan/pallas_call | solution.py:262
  19.2 61.0 %conditional.1 = (bf16[3,512,512]{2,1,0:T(8,128)(2,1)S(1)}) conditional(s32[]{:T(128)} %bitcast.1, (s32[16,128]{1,0:T(8,128)S(1)}, bf16[24,64,512]{2,1,0:T(8,128)(2,1)}) %tuple.25, (s32[16,128]{1,0:T(8,128)S(1)}, bf16[24,64,512]{2,1,0:T(8,128)(2,1)}) %tuple.25, (s32[16,128]{1,0:T(8,128)S(1)}, ...), branch_computations={%region_0.0_spmd, %region_1.0_spmd, %region_2.0_spmd, %region_3.0_... | conditional | bytes 8 | solution.py:607
  19.3 60.8 %exchange_14_11.1 = bf16[3,512,512]{2,1,0:T(8,128)(2,1)S(1)} custom-call(s32[16,128]{1,0:T(8,128)S(1)} %get-tuple-element.37.table, bf16[24,64,512]{2,1,0:T(8,128)(2,1)} %get-tuple-element.38.grads), custom_call_target="tpu_custom_call" | custom-call | tf_op jit(solution)/shard_map/cond/branch_3_fun/exchange_14_11/pallas_call | solution.py:510
  80.3 13.4 %update.1 = (bf16[3,512,512]{2,1,0:T(8,128)(2,1)}, bf16[3,512,512]{2,1,0:T(8,128)(2,1)}, bf16[3,512,512]{2,1,0:T(8,128)(2,1)}) custom-call(s32[3]{0:T(128)} %flag_ref.1, bf16[3,512,512]{2,1,0:T(8,128)(2,1)S(1)} %get-tuple-element.50.grad_ref, bf16[3,512,512]{2,1,0:T(8,128)(2,1)} %left_ref.1, bf16[3,512,512]{2,1,0:T(8,128)(2,1)} %right_ref.1, ...), custom_call_target="tpu_custom_call" | custom-call | tf_op jit(solution)/shard_map/update/pallas_call | solution.py:592

commit v3 on v2

--- a/solution.py
+++ b/solution.py
@@ -191,7 +191,7 @@
 
 
 MESH = pl.DeviceIdType.MESH
-BUILDS = ((10, 9), (12, 9), (14, 9), (14, 11), (16, 11), (32, 16))
+BUILDS = ((12, 8), (12, 9), (14, 8), (14, 9), (14, 11), (16, 11), (20, 12), (32, 16))
 
 
 def along(axis, distance):

time: 93.8 us -> 91 us (0.970)
  the two profiles are of different devices: /device:TPU:1 before, /device:TPU:39 now
where the time goes in v3:
time: 91 us; the launch traced here: 90.6 us
  Pallas kernels  88.6 us (97%)
  between operations  1.28 us (1%)
    pallas_call x1, Pallas kernels, exchange(): pl.pallas_call(functools.partial(exchange_kernel, steps_z, steps_y), out_...  59.4 us
    pallas_call x1, Pallas kernels, make_plan(): pl.pallas_call(plan_kernel, out_shape=[jax.ShapeDtypeStruct((16, 128), jn...  15.8 us
    pallas_call x1, Pallas kernels, update(): pl.pallas_call(update_kernel, grid=(slots,), in_specs=[pl.BlockSpec(memor...  13.4 us

profile of v3, /device:TPU:39, one launch (start us, length us, event | category | flops | bytes accessed | tf_op | source)
XLA Modules:
  0.0 90.6 jit_solution(13150867505585610653)
XLA Ops:
  0.6 15.8 %plan.1 = (s32[16,128]{1,0:T(8,128)S(1)}, s32[1,1]{1,0:T(1,128)}) custom-call(s32[1,1,24]{2,1,0:T(1,128)} %bitcast.2), custom_call_target="tpu_custom_call" | custom-call | tf_op jit(solution)/shard_map/plan/pallas_call | solution.py:262
  17.1 60.1 %conditional.1 = (bf16[3,512,512]{2,1,0:T(8,128)(2,1)S(1)}) conditional(s32[]{:T(128)} %bitcast.1, (s32[16,128]{1,0:T(8,128)S(1)}, bf16[24,64,512]{2,1,0:T(8,128)(2,1)}) %tuple.31, (s32[16,128]{1,0:T(8,128)S(1)}, bf16[24,64,512]{2,1,0:T(8,128)(2,1)}) %tuple.31, (s32[16,128]{1,0:T(8,128)S(1)}, ...), branch_computations={%region_0.0_spmd, %region_1.0_spmd, %region_2.0_spmd, %region_3.0_... | conditional | bytes 8 | solution.py:607
  17.3 59.4 %exchange_14_11.1 = bf16[3,512,512]{2,1,0:T(8,128)(2,1)S(1)} custom-call(s32[16,128]{1,0:T(8,128)S(1)} %get-tuple-element.49.table, bf16[24,64,512]{2,1,0:T(8,128)(2,1)} %get-tuple-element.50.grads), custom_call_target="tpu_custom_call" | custom-call | tf_op jit(solution)/shard_map/cond/branch_4_fun/exchange_14_11/pallas_call | solution.py:510
  77.2 13.4 %update.1 = (bf16[3,512,512]{2,1,0:T(8,128)(2,1)}, bf16[3,512,512]{2,1,0:T(8,128)(2,1)}, bf16[3,512,512]{2,1,0:T(8,128)(2,1)}) custom-call(s32[3]{0:T(128)} %flag_ref.1, bf16[3,512,512]{2,1,0:T(8,128)(2,1)S(1)} %get-tuple-element.64.grad_ref, bf16[3,512,512]{2,1,0:T(8,128)(2,1)} %left_ref.1, bf16[3,512,512]{2,1,0:T(8,128)(2,1)} %right_ref.1, ...), custom_call_target="tpu_custom_call" | custom-call | tf_op jit(solution)/shard_map/update/pallas_call | solution.py:592
